TPU v7x, 256 devices: a whole 4x4x8 slice. The times are simulated.
256 devices in a mesh: mem: 64 (over z, y, core), rep: 4 (over x).
Axes of the slice: x: 4, y: 4, z: 8, core: 2. Of those that a mesh axis runs over, the one named last changes fastest.
Arguments:
- memory: bfloat16 [4, 131072, 512], P('rep', 'mem'), may hold values from -6 to 6
- endpoint_owner: int32 [4, 2, 16384, 2], P('rep', None, 'mem'), may hold values from 0 to 63, all different within a row; in each aligned block of 256 rows (0 to 255, 256 to 511, ..., all dimensions but the last counted through in order) at most 16 rows name the same one
- endpoint_row: int32 [4, 2, 16384, 2], P('rep', None, 'mem'), may hold values from 0 to 2047
- event_time: int32 [4, 2, 16384], P('rep', None, 'mem'), may hold values from 1024 to 2047
- neighbour_time: int32 [4, 2, 16384], P('rep', None, 'mem'), may hold values from 0 to 1023
- neighbour_feat: bfloat16 [4, 2, 16384, 512], P('rep', None, 'mem'), may hold values from -6 to 6
- neighbour_index: int32 [4, 2, 16384, 128], P('rep', None, 'mem'), may hold values from 0 to 255
- valid_length: int32 [4, 2, 16384], P('rep', None, 'mem'), may hold values from 1 to 128, as said below
- decay_rate: float32 [8], replicated, may hold values from 0.02 to 2
- w_query: bfloat16 [512, 512], replicated, may hold values from -0.25 to 0.25
- w_keyval: bfloat16 [512, 1024], replicated, may hold values from -0.25 to 0.25
- w_out: bfloat16 [512, 512], replicated, may hold values from -0.25 to 0.25
- gru_input: bfloat16 [512, 1536], replicated, may hold values from -0.25 to 0.25
- gru_hidden: bfloat16 [512, 1536], replicated, may hold values from -0.25 to 0.25
- cotangent: bfloat16 [4, 2, 16384, 512], P('rep', None, 'mem'), may hold values from -6 to 6
Outputs:
- new_memory: bfloat16 [4, 131072, 512], P('rep', 'mem')
- embeddings: bfloat16 [4, 2, 16384, 512], P('rep', None, 'mem')
- grad_query: float32 [512, 512], P('mem')
- grad_keyval: float32 [512, 1024], P('mem')
- grad_out: float32 [512, 512], P('mem')
Inputs may be any that keep to these rules, and one draw needn't show every extreme that they name: `endpoint_owner`: within the events of one device in one batch (aligned blocks of 256 events), no shard is named more than 16 times, some shard exactly 16 times; the two endpoints of an event lie on different shards. `neighbour_index`: an index into the 256 neighbour rows of the event's block; indices may repeat and each listed entry counts. `valid_length`: the first event of every block has 128 listed neighbours.
All inputs are finite; a program needn't handle non-finite values.
Results may differ from a plain program's by a relative error of at most 0.017.
Values may be sent and summed in bfloat16 or wider, within the bound.
A program may use at most 128 MiB of HBM per device.

v0:
```python
import functools
import math

import jax
import jax.numpy as jnp
from jax import lax
from jax.experimental import pallas as pl
from jax.experimental.pallas import tpu as pltpu
from jax.sharding import PartitionSpec as P

MESH = pl.DeviceIdType.MESH
BF = jnp.bfloat16
F32 = jnp.float32
I32 = jnp.int32
CAP = 16
PLANE = 8
GROUP = CAP * PLANE
HEADS = 8
NY = 4


def nn(a, b):
    return lax.dot_general(a, b, (((1,), (0,)), ((), ())), preferred_element_type=F32)


def nt(a, b):
    return lax.dot_general(a, b, (((1,), (1,)), ((), ())), preferred_element_type=F32)


def sigmoid(a):
    return 0.5 * jnp.tanh(0.5 * a) + 0.5


def iota(shape, axis):
    return lax.broadcasted_iota(I32, shape, axis)


def one_hot(mask):
    return jnp.where(mask, 1.0, 0.0).astype(BF)


def window(
    nx,
    owner_ref,
    row_ref,
    et_ref,
    nt_ref,
    vl_ref,
    decay_ref,
    nidx_ref,
    mem_ref,
    feat_ref,
    cot_ref,
    wq_ref,
    wkv_ref,
    wo_ref,
    gi_ref,
    gh_ref,
    newmem_ref,
    emb_ref,
    gq_ref,
    gkv_ref,
    go_ref,
    ids_out,
    ids_in,
    served,
    answered,
    outgoing,
    arrived,
    mem1,
    slot_ref,
    lane_ref,
    col_ref,
    pick_ref,
    rows_ref,
    upd_ref,
    idx_ref,
    mult_ref,
    elapsed_ref,
    kv_ref,
    kvt_ref,
    q_ref,
    datt_ref,
    att_ref,
    dq_ref,
    dkv_ref,
    ga_ref,
    gb_ref,
    h1,
    r1,
    h2,
    r2,
    h3,
    r3,
    h4,
    r4,
    fin,
    send_sem,
    recv_sem,
):
    n = ids_in.shape[0]
    nz = n // PLANE
    nodes, width = mem_ref.shape
    events = et_ref.shape[1]
    nbrs = nt_ref.shape[1]
    ends = 2 * events
    slots = n * CAP
    me = lax.axis_index("mem")
    x = lax.axis_index("rep")
    z = me // PLANE
    yc = me % PLANE
    y = yc // 2
    c = yc % 2

    barrier = pltpu.get_barrier_semaphore()

    @pl.loop(1, n)
    def _(k):
        pl.semaphore_signal(barrier, inc=1, device_id={"mem": (me + k) % n}, device_id_type=MESH)

    for k in range(1, nx):
        pl.semaphore_signal(barrier, inc=1, device_id={"rep": (x + k) % nx}, device_id_type=MESH)

    def group_at(i):
        h = (i + 1) // 2
        return nz // 2 + h * (1 - 2 * (i % 2))

    def start_group(src, dst, g, length, sem):
        @pl.loop(0, PLANE)
        def _(j):
            @pl.when(g * PLANE + j > 0)
            def _():
                q = g * PLANE + (j + yc) % PLANE
                other = (q + z * PLANE) % n
                mine = (me + n - (other // PLANE) * PLANE) % n
                pltpu.make_async_remote_copy(
                    src_ref=src.at[pl.ds(pl.multiple_of(q * length, length), length)],
                    dst_ref=dst.at[pl.ds(pl.multiple_of(mine * length, length), length)],
                    send_sem=send_sem.at[sem],
                    recv_sem=recv_sem.at[sem],
                    device_id={"mem": other},
                    device_id_type=MESH,
                ).start()

    def own_block(src, dst):
        here = pl.ds(pl.multiple_of(yc * CAP, CAP), CAP)
        dst[here, :] = src[here, :]

    def wait_sent(view, sem):
        pltpu.make_async_copy(view, view, send_sem.at[sem]).wait()

    def wait_got(view, sem):
        pltpu.make_async_copy(view, view, recv_sem.at[sem]).wait()

    before = one_hot(iota((ends, ends), 0) < iota((ends, ends), 1))
    for b in range(2):
        own = owner_ref[b : b + 1, :] - z * PLANE
        own = jnp.where(own < 0, own + n, own)
        marks = jnp.where(iota((n, ends), 0) == own, 1.0, 0.0)
        marks_bf = marks.astype(BF)
        rank = jnp.sum(nn(marks_bf, before) * marks, axis=0, keepdims=True).astype(I32)
        slot_ref[b : b + 1, :] = own * CAP + rank
        wanted = row_ref[b : b + 1, :] + 1
        here = (iota((128, ends), 0) % CAP) == rank
        high = jnp.where(here, (wanted // 64).astype(F32), 0.0).astype(BF)
        low = jnp.where(here, (wanted % 64).astype(F32), 0.0).astype(BF)
        found = nt(marks_bf, high) * 64.0 + nt(marks_bf, low)
        ids_out[:, :, b * 128 : (b + 1) * 128] = (found.astype(I32) - 1).reshape(n, 1, 128)

    pl.semaphore_wait(barrier, n - 1 + nx - 1)

    @pl.loop(0, nz)
    def _(i):
        start_group(ids_out, ids_in, group_at(i), 1, 0)

    ids_in[pl.ds(yc, 1)] = ids_out[pl.ds(yc, 1)]
    wait_got(ids_in.at[pl.ds(0, n - 1)], 0)
    wait_sent(ids_out.at[pl.ds(0, n - 1)], 0)

    for b in range(2):
        seen = ids_in[:, :, b * 128 : (b + 1) * 128].reshape(n, 128).astype(F32)
        mine = (iota((n, 128), 0) % PLANE) == (iota((n, 128), 1) // CAP)
        packed = jnp.sum(jnp.where(mine, seen, 0.0).reshape(nz, PLANE, 128), axis=1)
        for g in range(nz):
            row = packed[g : g + 1, :]
            lane_ref[b : b + 1, g * GROUP : (g + 1) * GROUP] = row.astype(I32)
            col_ref[b, g * GROUP : (g + 1) * GROUP, :] = jnp.broadcast_to(row, (128, 128)).T.astype(I32)

    def serve(b, source):
        per = 2 if nz % 2 == 0 else 1

        @pl.loop(0, nz // per)
        def _(i):
            groups = [group_at(per * i + t) for t in range(per)]
            places = [pl.ds(pl.multiple_of(g * GROUP, GROUP), GROUP) for g in groups]
            wanted = jnp.concatenate([col_ref[b, p, 0:1] for p in places], axis=0)
            pick = one_hot(wanted == iota((per * GROUP, nodes), 1))
            got = nn(pick, source[...]).astype(BF)
            for t in range(per):
                served[b, places[t], :] = got[t * GROUP : (t + 1) * GROUP]
            for t in range(per):
                start_group(served.at[b], answered.at[b], groups[t], CAP, 1 + b)

        own_block(served.at[b], answered.at[b])

    def prepare(b):
        kv = nn(feat_ref[b], wkv_ref[...]).astype(BF)
        kv_ref[b] = kv
        kvt_ref[b] = kv.T
        slot_col = jnp.broadcast_to(slot_ref[b : b + 1, :].astype(F32), (128, ends)).T.astype(I32)
        pick_ref[b] = one_hot(slot_col[:, 0:1] == iota((ends, slots), 1))
        since = jnp.broadcast_to(nt_ref[b : b + 1, :].astype(F32), (128, nbrs)).T
        elapsed_ref[b] = jnp.log(1.0 + (et_ref[b : b + 1, :].astype(F32) - since[:, 0:1]))
        listed = nidx_ref[b].astype(F32).T
        count = listed.shape[0]
        idx_ref[...] = jnp.where(iota((count, events), 0) < vl_ref[b : b + 1, :], listed, -1.0).astype(I32)
        step = min(64, nbrs)

        @pl.loop(0, nbrs // step)
        def _(k):
            place = iota((step, events), 0) + k * step

            def add(j, total):
                rows = idx_ref[pl.ds(pl.multiple_of(j * 8, 8), 8), :]
                for t in range(8):
                    total = total + jnp.where(place == rows[t : t + 1, :], 1.0, 0.0)
                return total

            mult_ref[b, pl.ds(pl.multiple_of(k * step, step), step), :] = lax.fori_loop(
                0, count // 8, add, jnp.zeros((step, events), F32)
            )

    def fetch(b):
        wait_got(answered.at[b, pl.ds(0, slots - CAP)], 1 + b)
        got = nn(pick_ref[b], answered[b]).astype(BF)
        rows_ref[b, 0] = got[:events]
        rows_ref[b, 1] = got[events:]

    def update(b):
        @pl.loop(0, 2)
        def _(k):
            state = rows_ref[b, k]
            partner = rows_ref[b, 1 - k]
            gates = nn(partner, gi_ref[:, : 2 * width]) + nn(state, gh_ref[:, : 2 * width])
            reset = sigmoid(gates[:, :width])
            keep = sigmoid(gates[:, width:])
            candidate = jnp.tanh(
                nn(partner, gi_ref[:, 2 * width :]) + reset * nn(state, gh_ref[:, 2 * width :])
            )
            upd_ref[pl.ds(pl.multiple_of(k * events, events), events), :] = (
                candidate + keep * (state.astype(F32) - candidate)
            ).astype(BF)

        per = 2 if nz % 2 == 0 else 1

        @pl.loop(0, nz // per)
        def _(i):
            groups = [group_at(per * i + t) for t in range(per)]
            place = jnp.concatenate([iota((GROUP, ends), 0) + g * GROUP for g in groups], axis=0)
            got = nn(one_hot(place == slot_ref[b : b + 1, :]), upd_ref[...]).astype(BF)
            for t in range(per):
                at = pl.ds(pl.multiple_of(groups[t] * GROUP, GROUP), GROUP)
                outgoing[b, at, :] = got[t * GROUP : (t + 1) * GROUP]
            for t in range(per):
                start_group(outgoing.at[b], arrived.at[b], groups[t], CAP, 3 + b)

        own_block(outgoing.at[b], arrived.at[b])

    def apply(b, source, target):
        wait_got(arrived.at[b, pl.ds(0, slots - CAP)], 3 + b)
        step = min(512, nodes)

        @pl.loop(0, nodes // step)
        def _(k):
            at = pl.ds(pl.multiple_of(k * step, step), step)
            marks = jnp.where(iota((step, slots), 0) + k * step == lane_ref[b : b + 1, :], 1.0, 0.0)
            counts = jnp.sum(marks, axis=1, keepdims=True)
            sums = nn(marks.astype(BF), arrived[b])
            mean = sums * (1.0 / jnp.maximum(counts, 1.0))
            target[at, :] = jnp.where(counts > 0, mean, source[at, :].astype(F32)).astype(BF)

    def attend(b):
        source = rows_ref[b, 0]
        cot = cot_ref[b]
        q_ref[...] = nn(source, wq_ref[...]).astype(BF)
        datt_ref[...] = nt(cot, wo_ref[...]).astype(BF)
        scale = 1.0 / math.sqrt(width // HEADS)
        half_width = width // HEADS

        @pl.loop(0, HEADS // 2)
        def _(pair):
            cols = pl.ds(pl.multiple_of(pair * 2 * half_width, 2 * half_width), 2 * half_width)
            vcols = pl.ds(pl.multiple_of(width + pair * 2 * half_width, 2 * half_width), 2 * half_width)
            keys = kv_ref[b, :, cols]
            values = kv_ref[b, :, vcols]
            q_pair = q_ref[:, cols]
            d_pair = datt_ref[:, cols]
            dk = jnp.zeros((nbrs, 2 * half_width), F32)
            dv = jnp.zeros((nbrs, 2 * half_width), F32)
            for half in range(2):
                head = 2 * pair + half
                lanes = one_hot(iota((1, 2 * half_width), 1) // half_width == half)
                q = q_pair * lanes
                d = d_pair * lanes
                mult = mult_ref[b]
                live = mult > 0
                logits = nt(keys, q) * scale - decay_ref[head] * elapsed_ref[b]
                top = jnp.max(jnp.where(live, logits, -1e30), axis=0, keepdims=True)
                weighted = mult * jnp.exp(jnp.where(live, logits - top, -1e30))
                weights = weighted * (1.0 / jnp.sum(weighted, axis=0, keepdims=True))
                w = weights.astype(BF)
                at = pl.ds(pl.multiple_of(head * half_width, half_width), half_width)
                vat = pl.ds(pl.multiple_of(width + head * half_width, half_width), half_width)
                att_ref[at, :] = nn(kvt_ref[b, vat, :], w).astype(BF)
                dw = nt(values, d)
                inner = jnp.sum(dw * weights, axis=0, keepdims=True)
                dl = (weights * (dw - inner) * scale).astype(BF)
                dq_ref[at, :] = nn(kvt_ref[b, at, :], dl).astype(BF)
                dv = dv + nn(w, d)
                dk = dk + nn(dl, q)
            dkv_ref[:, cols] = dk.astype(BF)
            dkv_ref[:, vcols] = dv.astype(BF)

        emb_ref[b] = (source.astype(F32) + nn(att_ref[...].T, wo_ref[...])).astype(BF)
        go = nn(att_ref[...], cot)
        gq = nn(source.T, dq_ref[...].T)
        gkv = nn(feat_ref[b].T, dkv_ref[...])
        if b == 0:
            ga_ref[:, :width] = gq
            ga_ref[:, width:] = go
            gb_ref[...] = gkv
        else:
            ga_ref[:, :width] += gq
            ga_ref[:, width:] += go
            gb_ref[...] += gkv

    part = 2 * width // n
    cut = 2 * width // nx

    def copy_to(src, dst, where, sem):
        pltpu.make_async_remote_copy(
            src_ref=src,
            dst_ref=dst,
            send_sem=send_sem.at[sem],
            recv_sem=recv_sem.at[sem],
            device_id=where,
            device_id_type=MESH,
        ).start()

    def reduce_core():
        share = part // 2

        @pl.loop(0, n)
        def _(d):
            zz = d // PLANE
            yy = (d % PLANE) // 2
            cc = d % 2
            rows = pl.ds(pl.multiple_of(d * share, share), share)
            block = jnp.concatenate([ga_ref[rows, :], gb_ref[rows, :]], axis=0).astype(BF)
            at = pl.ds(pl.multiple_of((yy * nz + zz) * part, part), part)
            for k in range(nx):
                h1[cc, k, at, :] = block[:, k * cut : (k + 1) * cut]

        copy_to(h1.at[1 - c], r1, {"mem": me + 1 - 2 * c}, 5)

    def reduce_x():
        wait_got(r1, 5)
        for k in range(nx):
            h2[k] = (h1[c, k].astype(F32) + r1[k].astype(F32)).astype(BF)
        for k in range(1, nx):
            copy_to(h2.at[(x + k) % nx], r2.at[k - 1], {"rep": (x + k) % nx}, 6)

    def reduce_y():
        total = h2[x].astype(F32)
        if nx > 1:
            wait_got(r2, 6)
            for k in range(nx - 1):
                total = total + r2[k].astype(F32)
        h3[...] = total.astype(BF)
        length = nz * part
        for k in range(1, NY):
            yy = (y + k) % NY
            copy_to(
                h3.at[pl.ds(pl.multiple_of(yy * length, length), length)],
                r3.at[k - 1],
                {"mem": z * PLANE + yy * 2 + c},
                7,
            )

    def reduce_z():
        length = nz * part
        wait_got(r3, 7)
        total = h3[pl.ds(pl.multiple_of(y * length, length), length), :].astype(F32)
        for k in range(NY - 1):
            total = total + r3[k].astype(F32)
        h4[...] = total.astype(BF)
        for k in range(1, nz):
            zz = (z + k) % nz
            copy_to(
                h4.at[pl.ds(pl.multiple_of(zz * part, part), part)],
                r4.at[k - 1],
                {"mem": zz * PLANE + yc},
                8,
            )

    def share_x():
        total = h4[pl.ds(pl.multiple_of(z * part, part), part), :].astype(F32)
        if nz > 1:
            wait_got(r4, 8)
            for k in range(nz - 1):
                total = total + r4[k].astype(F32)
        fin[x] = total
        for k in range(1, nx):
            copy_to(fin.at[x], fin.at[x], {"rep": (x + k) % nx}, 9)

    def finish():
        if nx > 1:
            wait_got(fin.at[pl.ds(0, nx - 1)], 9)
        share = part // 2
        whole = jnp.concatenate([fin[k] for k in range(nx)], axis=1)
        gq_ref[...] = whole[:share, :width]
        go_ref[...] = whole[:share, width:]
        gkv_ref[...] = whole[share:, :]

    serve(0, mem_ref)
    prepare(0)
    prepare(1)
    fetch(0)
    update(0)
    attend(0)
    apply(0, mem_ref, mem1)
    serve(1, mem1)
    fetch(1)
    update(1)
    attend(1)
    reduce_core()
    reduce_x()
    apply(1, mem1, newmem_ref)
    reduce_y()
    reduce_z()
    share_x()
    finish()

    for b in range(2):
        wait_sent(served.at[b, pl.ds(0, slots - CAP)], 1 + b)
        wait_sent(outgoing.at[b, pl.ds(0, slots - CAP)], 3 + b)
    wait_sent(r1, 5)
    if nx > 1:
        wait_sent(r2, 6)
        wait_sent(fin.at[pl.ds(0, nx - 1)], 9)
    wait_sent(r3, 7)
    if nz > 1:
        wait_sent(r4, 8)


def on_device(
    memory,
    endpoint_owner,
    endpoint_row,
    event_time,
    neighbour_time,
    neighbour_feat,
    neighbour_index,
    valid_length,
    decay_rate,
    w_query,
    w_keyval,
    w_out,
    gru_input,
    gru_hidden,
    cotangent,
):
    n = lax.axis_size("mem")
    nx = lax.axis_size("rep")
    nz = n // PLANE
    _, nodes, width = memory.shape
    batches, events = event_time.shape[1:]
    nbrs = neighbour_time.shape[2]
    listed = neighbour_index.shape[3]
    ends = 2 * events
    slots = n * CAP
    part = 2 * width // n
    cut = 2 * width // nx
    owner = endpoint_owner[0].transpose(0, 2, 1).reshape(batches, ends)
    row = endpoint_row[0].transpose(0, 2, 1).reshape(batches, ends)
    vmem = pl.BlockSpec(memory_space=pltpu.VMEM)
    shape = jax.ShapeDtypeStruct
    share = width // n
    new_memory, embeddings, gq, gkv, go = pl.pallas_call(
        functools.partial(window, nx),
        out_shape=(
            shape((nodes, width), BF),
            shape((batches, events, width), BF),
            shape((share, width), F32),
            shape((share, 2 * width), F32),
            shape((share, width), F32),
        ),
        in_specs=[vmem] * 5 + [pl.BlockSpec(memory_space=pltpu.SMEM)] + [vmem] * 9,
        out_specs=(vmem,) * 5,
        scratch_shapes=[
            pltpu.VMEM((n, 1, 256), I32),
            pltpu.VMEM((n, 1, 256), I32),
            pltpu.VMEM((batches, slots, width), BF),
            pltpu.VMEM((batches, slots, width), BF),
            pltpu.VMEM((batches, slots, width), BF),
            pltpu.VMEM((batches, slots, width), BF),
            pltpu.VMEM((nodes, width), BF),
            pltpu.VMEM((8, ends), I32),
            pltpu.VMEM((8, slots), I32),
            pltpu.VMEM((batches, slots, 128), I32),
            pltpu.VMEM((batches, ends, slots), BF),
            pltpu.VMEM((batches, 2, events, width), BF),
            pltpu.VMEM((ends, width), BF),
            pltpu.VMEM((listed, events), I32),
            pltpu.VMEM((batches, nbrs, events), F32),
            pltpu.VMEM((batches, nbrs, events), F32),
            pltpu.VMEM((batches, nbrs, 2 * width), BF),
            pltpu.VMEM((batches, 2 * width, nbrs), BF),
            pltpu.VMEM((events, width), BF),
            pltpu.VMEM((events, width), BF),
            pltpu.VMEM((width, events), BF),
            pltpu.VMEM((width, events), BF),
            pltpu.VMEM((nbrs, 2 * width), BF),
            pltpu.VMEM((width, 2 * width), F32),
            pltpu.VMEM((width, 2 * width), F32),
            pltpu.VMEM((2, nx, n // 2 * part, cut), BF),
            pltpu.VMEM((nx, n // 2 * part, cut), BF),
            pltpu.VMEM((nx, n // 2 * part, cut), BF),
            pltpu.VMEM((max(nx - 1, 1), n // 2 * part, cut), BF),
            pltpu.VMEM((n // 2 * part, cut), BF),
            pltpu.VMEM((NY - 1, nz * part, cut), BF),
            pltpu.VMEM((nz * part, cut), BF),
            pltpu.VMEM((max(nz - 1, 1), part, cut), BF),
            pltpu.VMEM((nx, part, cut), F32),
            pltpu.SemaphoreType.DMA((10,)),
            pltpu.SemaphoreType.DMA((10,)),
        ],
        compiler_params=pltpu.CompilerParams(
            collective_id=0, has_side_effects=True, vmem_limit_bytes=60 * 1024 * 1024
        ),
        name="window",
    )(
        owner,
        row,
        event_time[0],
        neighbour_time[0],
        valid_length[0],
        decay_rate,
        neighbour_index[0],
        memory[0],
        neighbour_feat[0],
        cotangent[0],
        w_query,
        w_keyval,
        w_out,
        gru_input,
        gru_hidden,
    )
    return (new_memory[None], embeddings[None], gq, gkv, go)


def solution(mesh):
    return jax.shard_map(
        on_device,
        mesh=mesh,
        in_specs=(
            P("rep", "mem", None),
            P("rep", None, "mem", None),
            P("rep", None, "mem", None),
            P("rep", None, "mem"),
            P("rep", None, "mem"),
            P("rep", None, "mem", None),
            P("rep", None, "mem", None),
            P("rep", None, "mem"),
            P(),
            P(),
            P(),
            P(),
            P(),
            P(),
            P("rep", None, "mem", None),
        ),
        out_specs=(
            P("rep", "mem", None),
            P("rep", None, "mem", None),
            P("mem", None),
            P("mem", None),
            P("mem", None),
        ),
        check_vma=False,
    )
```

profile of v0, /device:TPU:1, one launch (start us, length us, event | category | flops | bytes accessed | tf_op | source)
XLA Modules:
  0.0 163.1 jit_solution(9984999435645943983)
XLA Ops:
  0.6 1.3 copy.20
  1.9 1.3 copy.21
  3.2 154.1 %window.1 = (bf16[2048,512]{1,0:T(8,128)(2,1)}, bf16[2,256,512]{2,1,0:T(8,128)(2,1)}, f32[8,512]{1,0:T(8,128)}, f32[8,1024]{1,0:T(8,128)}, f32[8,512]{1,0:T(8,128)}) custom-call(s32[2,512]{1,0:T(2,128)} %bitcast.25, s32[2,512]{1,0:T(2,128)} %bitcast.26, s32[2,256]{1,0:T(2,128)} %bitcast.29, s32[2,256]{1,0:T(2,128)} %bitcast.30, s32[2,256]{1,0:T(2,128)} %bitcast.31, ...), custom_call_target="tpu_custom_call" | custom-call | tf_op jit(solution)/shard_map/window/pallas_call | solution.py:489
  157.3 0.0 copy-start
  157.3 0.0 copy-start.3
  157.3 0.0 copy-start.1
  157.3 0.0 copy-start.2
  157.3 3.1 %copy.27 = bf16[1,2048,512]{2,1,0:T(8,128)(2,1)} copy(bf16[1,2048,512]{2,1,0:T(8,128)(2,1)} %bitcast.19) | data formatting | bytes 4194304
  160.4 0.0 copy-done
  160.4 0.8 copy.28
  161.2 0.0 copy-done.3
  161.2 0.6 copy.29
  161.8 0.0 copy-done.1
  161.8 0.6 copy.30
  162.4 0.0 copy-done.2
  162.5 0.6 copy.31
Async XLA Ops:
  157.3 3.1 %copy-start = (bf16[2,256,512]{2,1,0:T(8,128)(2,1)S(1)}, bf16[2,256,512]{2,1,0:T(8,128)(2,1)}, u32[]{:S(2)}) copy-start(bf16[2,256,512]{2,1,0:T(8,128)(2,1)} %get-tuple-element.11) | copy-start | bytes 1572868
  157.3 3.9 %copy-start.3 = (f32[8,512]{1,0:T(8,128)S(1)}, f32[8,512]{1,0:T(8,128)}, u32[]{:S(2)}) copy-start(f32[8,512]{1,0:T(8,128)} %get-tuple-element.22) | copy-start | bytes 49156
  157.3 4.5 %copy-start.1 = (f32[8,1024]{1,0:T(8,128)S(1)}, f32[8,1024]{1,0:T(8,128)}, u32[]{:S(2)}) copy-start(f32[8,1024]{1,0:T(8,128)} %get-tuple-element.23) | copy-start | bytes 98308
  157.3 5.1 %copy-start.2 = (f32[8,512]{1,0:T(8,128)S(1)}, f32[8,512]{1,0:T(8,128)}, u32[]{:S(2)}) copy-start(f32[8,512]{1,0:T(8,128)} %get-tuple-element.24) | copy-start | bytes 49156
where the time goes:
time: 164 us; the launch traced here: 163 us
  Pallas kernels  154 us (94%)
  local copies, waits for them, and re-layouts  8.29 us (5%)
    pallas_call x1, Pallas kernels, on_device(): pl.pallas_call(functools.partial(window, nx), out_shape=(shape((nodes, wi...  154 us
    unnamed x15, local copies, waits for them, and re-layouts  8.29 us

commit v1 on v0

v1 whole, which is shorter than its diff:
```python
import functools
import math

import jax
import jax.numpy as jnp
from jax import lax
from jax.experimental import pallas as pl
from jax.experimental.pallas import tpu as pltpu
from jax.sharding import PartitionSpec as P

MESH = pl.DeviceIdType.MESH
BF = jnp.bfloat16
F32 = jnp.float32
I32 = jnp.int32
CAP = 16
PLANE = 8
GROUP = CAP * PLANE
HEADS = 8
NY = 4


def nn(a, b):
    return lax.dot_general(a, b, (((1,), (0,)), ((), ())), preferred_element_type=F32)


def nt(a, b):
    return lax.dot_general(a, b, (((1,), (1,)), ((), ())), preferred_element_type=F32)


def sigmoid(a):
    return 0.5 * jnp.tanh(0.5 * a) + 0.5


def iota(shape, axis):
    return lax.broadcasted_iota(I32, shape, axis)


def one_hot(mask):
    return jnp.where(mask, 1.0, 0.0).astype(BF)


def window(
    nx,
    owner_ref,
    row_ref,
    et_ref,
    nt_ref,
    vl_ref,
    decay_ref,
    nidx_hbm,
    mem_hbm,
    feat_hbm,
    cot_hbm,
    wq_hbm,
    wkv_hbm,
    wo_hbm,
    gi_hbm,
    gh_hbm,
    newmem_hbm,
    emb_hbm,
    gq_ref,
    gkv_ref,
    go_ref,
    nidx_ref,
    mem_ref,
    feat_ref,
    cot_ref,
    wq_ref,
    wkv_ref,
    wo_ref,
    gi_ref,
    gh_ref,
    newmem_ref,
    emb_ref,
    in_sem,
    out_sem,
    ids_out,
    ids_in,
    served,
    answered,
    outgoing,
    arrived,
    mem1,
    slot_ref,
    lane_ref,
    col_ref,
    pick_ref,
    pickt_ref,
    asked_ref,
    named_ref,
    inverse_ref,
    rows_ref,
    upd_ref,
    idx_ref,
    mult_ref,
    bias_ref,
    dw_ref,
    kv_ref,
    kvt_ref,
    q_ref,
    datt_ref,
    att_ref,
    dq_ref,
    dkv_ref,
    ga_ref,
    gb_ref,
    h1,
    r1,
    h2,
    r2,
    h3,
    r3,
    h4,
    r4,
    send_sem,
    recv_sem,
):
    n = ids_in.shape[0]
    nz = n // PLANE
    nodes, width = mem_ref.shape
    events = et_ref.shape[1]
    nbrs = nt_ref.shape[1]
    ends = 2 * events
    slots = n * CAP
    wide = width // 2
    me = lax.axis_index("mem")
    x = lax.axis_index("rep")
    z = me // PLANE
    yc = me % PLANE
    y = yc // 2
    c = yc % 2

    loads = {}
    for at, (name, src, dst) in enumerate(
        (
            ("mem", mem_hbm, mem_ref),
            ("nidx", nidx_hbm, nidx_ref),
            ("feat", feat_hbm, feat_ref),
            ("wkv", wkv_hbm, wkv_ref),
            ("gi", gi_hbm, gi_ref),
            ("gh", gh_hbm, gh_ref),
            ("wq", wq_hbm, wq_ref),
            ("wo", wo_hbm, wo_ref),
            ("cot", cot_hbm, cot_ref),
        )
    ):
        loads[name] = pltpu.make_async_copy(src, dst, in_sem.at[at])
        loads[name].start()

    def loaded(*names):
        for name in names:
            loads[name].wait()

    barrier = pltpu.get_barrier_semaphore()

    @pl.loop(1, n)
    def _(k):
        pl.semaphore_signal(barrier, inc=1, device_id={"mem": (me + k) % n}, device_id_type=MESH)

    for k in range(1, nx):
        pl.semaphore_signal(barrier, inc=1, device_id={"rep": (x + k) % nx}, device_id_type=MESH)

    @pl.loop(1, nz)
    def _(k):
        for j in range(1, nx):
            pl.semaphore_signal(
                barrier,
                inc=1,
                device_id={"mem": (z + k) % nz * PLANE + yc, "rep": (x + j) % nx},
                device_id_type=MESH,
            )

    def group_at(i):
        h = (i + 1) // 2
        return nz // 2 + h * (1 - 2 * (i % 2))

    def start_group(src, dst, g, sem):
        @pl.loop(0, PLANE)
        def _(j):
            @pl.when(g * PLANE + j > 0)
            def _():
                q = g * PLANE + (j + yc) % PLANE
                other = (q + z * PLANE) % n
                mine = (me + n - (other // PLANE) * PLANE) % n
                pltpu.make_async_remote_copy(
                    src_ref=src(q),
                    dst_ref=dst(mine),
                    send_sem=send_sem.at[sem],
                    recv_sem=recv_sem.at[sem],
                    device_id={"mem": other},
                    device_id_type=MESH,
                ).start()

    def columns(t):
        return pl.ds(t * wide, wide)

    def block(ref, b, t):
        return lambda q: ref.at[b, pl.ds(pl.multiple_of(q * CAP, CAP), CAP), columns(t)]

    def own_block(src, dst, b, t):
        here = pl.ds(pl.multiple_of(yc * CAP, CAP), CAP)
        dst[b, here, columns(t)] = src[b, here, columns(t)]

    def others(ref, b, t):
        return ref.at[b, pl.ds(0, slots - CAP), columns(t)]

    def wait_sent(view, sem):
        pltpu.make_async_copy(view, view, send_sem.at[sem]).wait()

    def wait_got(view, sem):
        pltpu.make_async_copy(view, view, recv_sem.at[sem]).wait()

    before = one_hot(iota((ends, ends), 0) < iota((ends, ends), 1))
    for b in range(2):
        own = jnp.concatenate([owner_ref[b, 0:1, :], owner_ref[b, 1:2, :]], axis=1) - z * PLANE
        own = jnp.where(own < 0, own + n, own)
        marks = jnp.where(iota((n, ends), 0) == own, 1.0, 0.0)
        marks_bf = marks.astype(BF)
        rank = jnp.sum(nn(marks_bf, before) * marks, axis=0, keepdims=True).astype(I32)
        slot_ref[b : b + 1, :] = own * CAP + rank
        wanted = jnp.concatenate([row_ref[b, 0:1, :], row_ref[b, 1:2, :]], axis=1) + 1
        here = (iota((128, ends), 0) % CAP) == rank
        high = jnp.where(here, (wanted // 64).astype(F32), 0.0).astype(BF)
        low = jnp.where(here, (wanted % 64).astype(F32), 0.0).astype(BF)
        found = nt(marks_bf, high) * 64.0 + nt(marks_bf, low)
        ids_out[:, :, b * 128 : (b + 1) * 128] = (found.astype(I32) - 1).reshape(n, 1, 128)

    pl.semaphore_wait(barrier, n - 1 + (nx - 1) * nz)

    @pl.loop(0, nz)
    def _(i):
        start_group(lambda q: ids_out.at[pl.ds(q, 1)], lambda q: ids_in.at[pl.ds(q, 1)], group_at(i), 0)

    ids_in[pl.ds(yc, 1)] = ids_out[pl.ds(yc, 1)]
    wait_got(ids_in.at[pl.ds(0, n - 1)], 0)
    wait_sent(ids_out.at[pl.ds(0, n - 1)], 0)

    for b in range(2):
        seen = ids_in[:, :, b * 128 : (b + 1) * 128].reshape(n, 128).astype(F32)
        mine = (iota((n, 128), 0) % PLANE) == (iota((n, 128), 1) // CAP)
        packed = jnp.sum(jnp.where(mine, seen, 0.0).reshape(nz, PLANE, 128), axis=1)
        for g in range(nz):
            row = packed[g : g + 1, :]
            lane_ref[b : b + 1, g * GROUP : (g + 1) * GROUP] = row.astype(I32)
            col_ref[b, g * GROUP : (g + 1) * GROUP, :] = jnp.broadcast_to(row, (128, 128)).T.astype(I32)

    per = 2 if nz % 2 == 0 else 1

    def places(i):
        groups = [group_at(per * i + t) for t in range(per)]
        return groups, [pl.ds(pl.multiple_of(g * GROUP, GROUP), GROUP) for g in groups]

    def ask(b, where):
        wanted = jnp.concatenate([col_ref[b, at, 0:1] for at in where], axis=0)
        pick = one_hot(wanted == iota((per * GROUP, nodes), 1))
        for t in range(per):
            asked_ref[where[t], :] = pick[t * GROUP : (t + 1) * GROUP]
        return pick

    def ask_all(b):
        @pl.loop(0, nz // per)
        def _(i):
            ask(b, places(i)[1])

    def serve(b, t, source):
        @pl.loop(0, nz // per)
        def _(i):
            groups, where = places(i)
            if b == 0 and t == 0:
                pick = ask(b, where)
            else:
                pick = jnp.concatenate([asked_ref[at, :] for at in where], axis=0)
            got = nn(pick, source[:, columns(t)]).astype(BF)
            for k in range(per):
                served[b, where[k], columns(t)] = got[k * GROUP : (k + 1) * GROUP]
            for k in range(per):
                start_group(block(served, b, t), block(answered, b, t), groups[k], 1 + 2 * b + t)

        own_block(served, answered, b, t)

    def prepare(b):
        kv = nn(feat_ref[b], wkv_ref[...]).astype(BF)
        kv_ref[...] = kv
        kvt_ref[...] = kv.T
        datt_ref[...] = nt(cot_ref[b], wo_ref[...]).astype(BF)
        slot_row = slot_ref[b : b + 1, :]
        slot_col = jnp.broadcast_to(slot_row.astype(F32), (128, ends)).T.astype(I32)
        pick_ref[...] = one_hot(slot_col[:, 0:1] == iota((ends, slots), 1))
        pickt_ref[...] = one_hot(iota((slots, ends), 0) == slot_row)
        listed = nidx_ref[b].astype(F32).T
        count = listed.shape[0]
        idx_ref[...] = jnp.where(iota((count, events), 0) < vl_ref[b : b + 1, :], listed, -1.0).astype(I32)
        step = min(64, nbrs)

        @pl.loop(0, nbrs // step)
        def _(k):
            place = iota((step, events), 0) + k * step

            def add(j, total):
                rows = idx_ref[pl.ds(pl.multiple_of(j * 8, 8), 8), :]
                for t in range(8):
                    total = total + jnp.where(place == rows[t : t + 1, :], 1.0, 0.0)
                return total

            mult_ref[pl.ds(pl.multiple_of(k * step, step), step), :] = lax.fori_loop(
                0, count // 8, add, jnp.zeros((step, events), F32)
            )

        since = jnp.broadcast_to(nt_ref[b : b + 1, :].astype(F32), (128, nbrs)).T
        elapsed = jnp.log(1.0 + (et_ref[b : b + 1, :].astype(F32) - since[:, 0:1]))
        mult = mult_ref[...]
        level = jnp.where(mult > 0, jnp.log(jnp.maximum(mult, 1.0)), -1e30)
        for head in range(HEADS):
            bias_ref[head] = level - decay_ref[head] * elapsed
            d = datt_ref[:, pair_columns(head // 2)] * half_lanes(head % 2, 1.0)
            dw_ref[head] = nt(kv_ref[:, pair_columns(head // 2, width)], d)

    half_width = width // HEADS

    def pair_columns(pair, base=0):
        return pl.ds(base + pair * 2 * half_width, 2 * half_width)

    def half_lanes(half, value):
        return jnp.where(iota((1, 2 * half_width), 1) // half_width == half, value, 0.0).astype(BF)

    step = min(512, nodes)

    def name_rows(b):
        @pl.loop(0, nodes // step)
        def _(k):
            at = pl.ds(pl.multiple_of(k * step, step), step)
            marks = jnp.where(iota((step, slots), 0) + k * step == lane_ref[b : b + 1, :], 1.0, 0.0)
            counts = jnp.sum(marks, axis=1, keepdims=True)
            named_ref[at, :] = marks.astype(BF)
            inverse = jnp.where(counts > 0, 1.0 / jnp.maximum(counts, 1.0), 0.0)
            inverse_ref[at, :] = jnp.broadcast_to(inverse, (step, 128))

    def fetch(b):
        for t in range(2):
            wait_got(others(answered, b, t), 1 + 2 * b + t)
            got = nn(pick_ref[...], answered[b, :, columns(t)]).astype(BF)
            rows_ref[b, 0, :, columns(t)] = got[:events]
            rows_ref[b, 1, :, columns(t)] = got[events:]

    def update(b):
        for t in range(2):

            @pl.loop(0, 2)
            def _(k):
                state = rows_ref[b, k]
                partner = rows_ref[b, 1 - k]
                part = [slice(i * width + t * wide, i * width + (t + 1) * wide) for i in range(3)]
                reset = sigmoid(nn(partner, gi_ref[:, part[0]]) + nn(state, gh_ref[:, part[0]]))
                keep = sigmoid(nn(partner, gi_ref[:, part[1]]) + nn(state, gh_ref[:, part[1]]))
                candidate = jnp.tanh(nn(partner, gi_ref[:, part[2]]) + reset * nn(state, gh_ref[:, part[2]]))
                old = rows_ref[b, k, :, columns(t)].astype(F32)
                upd_ref[pl.ds(pl.multiple_of(k * events, events), events), columns(t)] = (
                    candidate + keep * (old - candidate)
                ).astype(BF)

            @pl.loop(0, nz // per)
            def _(i):
                groups, where = places(i)
                pick = jnp.concatenate([pickt_ref[at, :] for at in where], axis=0)
                got = nn(pick, upd_ref[:, columns(t)]).astype(BF)
                for k in range(per):
                    outgoing[b, where[k], columns(t)] = got[k * GROUP : (k + 1) * GROUP]
                for k in range(per):
                    start_group(block(outgoing, b, t), block(arrived, b, t), groups[k], 5 + 2 * b + t)

            own_block(outgoing, arrived, b, t)

    def apply(b, t, source, target):
        wait_got(others(arrived, b, t), 5 + 2 * b + t)

        @pl.loop(0, nodes // step)
        def _(k):
            at = pl.ds(pl.multiple_of(k * step, step), step)
            sums = nn(named_ref[at, :], arrived[b, :, columns(t)])
            inverse = inverse_ref[at, 0:1]
            old = source[at, columns(t)].astype(F32)
            target[at, columns(t)] = jnp.where(inverse > 0, sums * inverse, old).astype(BF)

    def store_memory(k):
        at = pl.ds(k * step, step)
        return pltpu.make_async_copy(newmem_ref.at[at], newmem_hbm.at[at], out_sem.at[2 + k])

    def store_embeddings(b):
        return pltpu.make_async_copy(emb_ref.at[b], emb_hbm.at[b], out_sem.at[b])

    def attend(b):
        source = rows_ref[b, 0]
        cot = cot_ref[b]
        q_ref[...] = nn(source, wq_ref[...]).astype(BF)
        scale = 1.0 / math.sqrt(half_width)

        for pair in range(HEADS // 2):
            cols = pair_columns(pair)
            vcols = pair_columns(pair, width)
            dk = jnp.zeros((nbrs, 2 * half_width), F32)
            dv = jnp.zeros((nbrs, 2 * half_width), F32)
            for half in range(2):
                head = 2 * pair + half
                q = q_ref[:, cols] * half_lanes(half, scale)
                d = datt_ref[:, cols] * half_lanes(half, 1.0)
                logits = nt(kv_ref[:, cols], q) + bias_ref[head]
                weighted = jnp.exp(logits - jnp.max(logits, axis=0, keepdims=True))
                weights = weighted * (1.0 / jnp.sum(weighted, axis=0, keepdims=True))
                w = weights.astype(BF)
                at = pl.ds(head * half_width, half_width)
                vat = pl.ds(width + head * half_width, half_width)
                att_ref[at, :] = nn(kvt_ref[vat, :], w).astype(BF)
                dw = dw_ref[head]
                inner = jnp.sum(dw * weights, axis=0, keepdims=True)
                dl = (weights * (dw - inner)).astype(BF)
                dq_ref[at, :] = (nn(kvt_ref[at, :], dl) * scale).astype(BF)
                dv = dv + nn(w, d)
                dk = dk + nn(dl, q)
            dkv_ref[:, cols] = dk.astype(BF)
            dkv_ref[:, vcols] = dv.astype(BF)

        emb_ref[b] = (source.astype(F32) + nn(att_ref[...].T, wo_ref[...])).astype(BF)
        go = nn(att_ref[...], cot)
        gq = nn(source.T, dq_ref[...].T)
        gkv = nn(feat_ref[b].T, dkv_ref[...])
        if b == 0:
            ga_ref[:, :width] = gq
            ga_ref[:, width:] = go
            gb_ref[...] = gkv
        else:
            ga_ref[:, :width] += gq
            ga_ref[:, width:] += go
            gb_ref[...] += gkv

    part = 2 * width // n
    plane = nz * part
    cut = width // nx

    def copy_to(src, dst, where, sem):
        pltpu.make_async_remote_copy(
            src_ref=src,
            dst_ref=dst,
            send_sem=send_sem.at[sem],
            recv_sem=recv_sem.at[sem],
            device_id=where,
            device_id_type=MESH,
        ).start()

    def rows_of_y(k):
        return pl.ds(pl.multiple_of(k * plane, plane), plane)

    def rows_of_z(k):
        return pl.ds(pl.multiple_of(k * part, part), part)

    def reduce_core(t):
        share = part // 2

        @pl.loop(0, n)
        def _(d):
            zz = d // PLANE
            yy = (d % PLANE) // 2
            cc = d % 2
            rows = pl.ds(pl.multiple_of(d * share, share), share)
            cols = pl.ds(t * width, width)
            both = jnp.concatenate([ga_ref[rows, cols], gb_ref[rows, cols]], axis=0).astype(BF)
            at = pl.ds(pl.multiple_of((yy * nz + zz) * part, part), part)
            for k in range(nx):
                h1[t, cc, k, at, :] = both[:, k * cut : (k + 1) * cut]

        copy_to(h1.at[t, 1 - c], r1.at[t], {"mem": me + 1 - 2 * c}, 9 + t)

    def reduce_x(t):
        wait_got(r1.at[t], 9 + t)
        for k in range(nx):
            h2[t, k] = (h1[t, c, k].astype(F32) + r1[t, k].astype(F32)).astype(BF)
        for k in range(1, nx):
            xx = (x + k) % nx
            copy_to(h2.at[t, xx], r2.at[t, k - 1], {"rep": xx}, 11 + t)

    def reduce_y(t):
        total = h2[t, x].astype(F32)
        if nx > 1:
            wait_got(r2.at[t], 11 + t)
            for k in range(nx - 1):
                total = total + r2[t, k].astype(F32)
        h3[t] = total.astype(BF)
        for k in range(1, NY):
            yy = (y + k) % NY
            copy_to(h3.at[t, rows_of_y(yy)], r3.at[t, k - 1], {"mem": z * PLANE + yy * 2 + c}, 13 + t)

    def reduce_z():
        for t in range(2):
            wait_got(r3.at[t], 13 + t)
            total = h3[t, rows_of_y(y), :].astype(F32)
            for k in range(NY - 1):
                total = total + r3[t, k].astype(F32)
            h4[:, t * cut : (t + 1) * cut] = total.astype(BF)
        here = r4.at[z * nx + x]
        here[...] = h4[rows_of_z(z), :]
        for k in range(1, nx):
            copy_to(h4.at[rows_of_z(z)], here, {"rep": (x + k) % nx}, 15)

        @pl.loop(1, nz)
        def _(k):
            zz = (z + k) % nz
            for j in range(nx):
                there = {"mem": zz * PLANE + yc, "rep": (x + j) % nx} if j else {"mem": zz * PLANE + yc}
                copy_to(h4.at[rows_of_z(zz)], here, there, 15)

    def all_but_one():
        return r4.at[pl.ds(0, nz * nx - 1)]

    def finish():
        wait_got(all_but_one(), 15)
        share = part // 2
        for k in range(nx):
            total = r4[k].astype(F32)
            for j in range(1, nz):
                total = total + r4[j * nx + k].astype(F32)
            at = slice(k * cut, (k + 1) * cut)
            gq_ref[:, at] = total[:share, :cut]
            go_ref[:, at] = total[:share, cut:]
            gkv_ref[:, at] = total[share:, :cut]
            gkv_ref[:, width + k * cut : width + (k + 1) * cut] = total[share:, cut:]

    loaded("mem")
    serve(0, 0, mem_ref)
    serve(0, 1, mem_ref)
    loaded("nidx", "feat", "wkv", "wo", "cot")
    prepare(0)
    name_rows(0)
    ask_all(1)
    loaded("gi", "gh", "wq")
    fetch(0)
    update(0)
    attend(0)
    store_embeddings(0).start()
    for t in range(2):
        apply(0, t, mem_ref, mem1)
        serve(1, t, mem1)
    prepare(1)
    name_rows(1)
    fetch(1)
    update(1)
    attend(1)
    store_embeddings(1).start()
    reduce_core(0)
    reduce_core(1)
    reduce_x(0)
    reduce_x(1)
    apply(1, 0, mem1, newmem_ref)
    reduce_y(0)
    reduce_y(1)
    reduce_z()
    apply(1, 1, mem1, newmem_ref)
    for k in range(nodes // step):
        store_memory(k).start()
    finish()

    for b in range(2):
        for t in range(2):
            wait_sent(others(served, b, t), 1 + 2 * b + t)
            wait_sent(others(outgoing, b, t), 5 + 2 * b + t)
        store_embeddings(b).wait()
    for t in range(2):
        wait_sent(r1.at[t], 9 + t)
        if nx > 1:
            wait_sent(r2.at[t], 11 + t)
        wait_sent(r3.at[t], 13 + t)
    wait_sent(all_but_one(), 15)
    for k in range(nodes // step):
        store_memory(k).wait()


def hand_on(*refs):
    count = (len(refs) - 1) // 3
    sem = refs[-1]
    steps = []
    for src, dst, held in zip(refs[:count], refs[count : 2 * count], refs[2 * count : 3 * count]):
        rows = src.shape[0]
        pieces = 4 if rows % 128 == 0 else 1
        for k in range(pieces):
            at = pl.ds(k * (rows // pieces), rows // pieces)
            get = pltpu.make_async_copy(src.at[at], held.at[at], sem.at[0, len(steps)])
            put = pltpu.make_async_copy(held.at[at], dst.at[at], sem.at[1, len(steps)])
            get.start()
            steps.append((get, put))
    for get, put in steps:
        get.wait()
        put.start()
    for _, put in steps:
        put.wait()


def on_device(
    memory,
    endpoint_owner,
    endpoint_row,
    event_time,
    neighbour_time,
    neighbour_feat,
    neighbour_index,
    valid_length,
    decay_rate,
    w_query,
    w_keyval,
    w_out,
    gru_input,
    gru_hidden,
    cotangent,
):
    n = lax.axis_size("mem")
    nx = lax.axis_size("rep")
    nz = n // PLANE
    _, nodes, width = memory.shape
    batches, events = event_time.shape[1:]
    nbrs = neighbour_time.shape[2]
    listed = neighbour_index.shape[3]
    ends = 2 * events
    slots = n * CAP
    part = 2 * width // n
    plane = nz * part
    half = n // 2 * part
    cut = width // nx
    owner = endpoint_owner[0].transpose(0, 2, 1)
    row = endpoint_row[0].transpose(0, 2, 1)
    vmem = pl.BlockSpec(memory_space=pltpu.VMEM)
    shape = jax.ShapeDtypeStruct
    share = width // n
    hbm = pl.BlockSpec(memory_space=pl.ANY)
    outputs = (
        shape((nodes, width), BF),
        shape((batches, events, width), BF),
        shape((share, width), F32),
        shape((share, 2 * width), F32),
        shape((share, width), F32),
    )
    results = pl.pallas_call(
        functools.partial(window, nx),
        out_shape=outputs,
        in_specs=[vmem] * 5 + [pl.BlockSpec(memory_space=pltpu.SMEM)] + [hbm] * 9,
        out_specs=(hbm,) * 2 + (vmem,) * 3,
        scratch_shapes=[
            pltpu.VMEM((batches, events, listed), I32),
            pltpu.VMEM((nodes, width), BF),
            pltpu.VMEM((batches, nbrs, width), BF),
            pltpu.VMEM((batches, events, width), BF),
            pltpu.VMEM((width, width), BF),
            pltpu.VMEM((width, 2 * width), BF),
            pltpu.VMEM((width, width), BF),
            pltpu.VMEM((width, 3 * width), BF),
            pltpu.VMEM((width, 3 * width), BF),
            pltpu.VMEM((nodes, width), BF),
            pltpu.VMEM((batches, events, width), BF),
            pltpu.SemaphoreType.DMA((9,)),
            pltpu.SemaphoreType.DMA((2 + nodes // min(512, nodes),)),
            pltpu.VMEM((n, 1, 256), I32),
            pltpu.VMEM((n, 1, 256), I32),
            pltpu.VMEM((batches, slots, width), BF),
            pltpu.VMEM((batches, slots, width), BF),
            pltpu.VMEM((batches, slots, width), BF),
            pltpu.VMEM((batches, slots, width), BF),
            pltpu.VMEM((nodes, width), BF),
            pltpu.VMEM((8, ends), I32),
            pltpu.VMEM((8, slots), I32),
            pltpu.VMEM((batches, slots, 128), I32),
            pltpu.VMEM((ends, slots), BF),
            pltpu.VMEM((slots, ends), BF),
            pltpu.VMEM((slots, nodes), BF),
            pltpu.VMEM((nodes, slots), BF),
            pltpu.VMEM((nodes, 128), F32),
            pltpu.VMEM((batches, 2, events, width), BF),
            pltpu.VMEM((ends, width), BF),
            pltpu.VMEM((listed, events), I32),
            pltpu.VMEM((nbrs, events), F32),
            pltpu.VMEM((HEADS, nbrs, events), F32),
            pltpu.VMEM((HEADS, nbrs, events), F32),
            pltpu.VMEM((nbrs, 2 * width), BF),
            pltpu.VMEM((2 * width, nbrs), BF),
            pltpu.VMEM((events, width), BF),
            pltpu.VMEM((events, width), BF),
            pltpu.VMEM((width, events), BF),
            pltpu.VMEM((width, events), BF),
            pltpu.VMEM((nbrs, 2 * width), BF),
            pltpu.VMEM((width, 2 * width), F32),
            pltpu.VMEM((width, 2 * width), F32),
            pltpu.VMEM((2, 2, nx, half, cut), BF),
            pltpu.VMEM((2, nx, half, cut), BF),
            pltpu.VMEM((2, nx, half, cut), BF),
            pltpu.VMEM((2, max(nx - 1, 1), half, cut), BF),
            pltpu.VMEM((2, half, cut), BF),
            pltpu.VMEM((2, NY - 1, plane, cut), BF),
            pltpu.VMEM((plane, 2 * cut), BF),
            pltpu.VMEM((nz * nx, part, 2 * cut), BF),
            pltpu.SemaphoreType.DMA((16,)),
            pltpu.SemaphoreType.DMA((16,)),
        ],
        compiler_params=pltpu.CompilerParams(
            collective_id=0, has_side_effects=True, vmem_limit_bytes=60 * 1024 * 1024
        ),
        name="window",
    )(
        owner,
        row,
        event_time[0],
        neighbour_time[0],
        valid_length[0],
        decay_rate,
        neighbour_index[0],
        memory[0],
        neighbour_feat[0],
        cotangent[0],
        w_query,
        w_keyval,
        w_out,
        gru_input,
        gru_hidden,
    )
    new_memory, embeddings, gq, gkv, go = pl.pallas_call(
        hand_on,
        out_shape=outputs,
        in_specs=[hbm] * 5,
        out_specs=(hbm,) * 5,
        scratch_shapes=[pltpu.VMEM(out.shape, out.dtype) for out in outputs] + [pltpu.SemaphoreType.DMA((2, 8))],
        compiler_params=pltpu.CompilerParams(vmem_limit_bytes=60 * 1024 * 1024),
        name="hand_on",
    )(*results)
    return (new_memory[None], embeddings[None], gq, gkv, go)


def solution(mesh):
    return jax.shard_map(
        on_device,
        mesh=mesh,
        in_specs=(
            P("rep", "mem", None),
            P("rep", None, "mem", None),
            P("rep", None, "mem", None),
            P("rep", None, "mem"),
            P("rep", None, "mem"),
            P("rep", None, "mem", None),
            P("rep", None, "mem", None),
            P("rep", None, "mem"),
            P(),
            P(),
            P(),
            P(),
            P(),
            P(),
            P("rep", None, "mem", None),
        ),
        out_specs=(
            P("rep", "mem", None),
            P("rep", None, "mem", None),
            P("mem", None),
            P("mem", None),
            P("mem", None),
        ),
        check_vma=False,
    )
```

time: 164 us -> 143 us (0.87)
  Pallas kernels: 154 us -> 142 us
  local copies, waits for them, and re-layouts: 8.29 us -> 0 us
    pallas_call x1 -> x2, Pallas kernels: 154 us -> 142 us  [the longest x1 139 us: on_device(): pl.pallas_call(functools.partial(window, nx), out_shape=outputs, in_specs...]
    unnamed x15 -> x0, local copies, waits for them, and re-layouts: 8.29 us -> none
where the time goes in v1:
time: 143 us
  Pallas kernels  142 us (99%)
    pallas_call x1, Pallas kernels, on_device(): pl.pallas_call(functools.partial(window, nx), out_shape=outputs, in_specs...  139 us

profile of v1, /device:TPU:1, one launch (start us, length us, event | category | flops | bytes accessed | tf_op | source)
XLA Modules:
  0.0 142.9 jit_solution(15062885258209151530)
XLA Ops:
  0.6 139.4 %window.1 = (bf16[2048,512]{1,0:T(8,128)(2,1)}, bf16[2,256,512]{2,1,0:T(8,128)(2,1)}, f32[8,512]{1,0:T(8,128)}, f32[8,1024]{1,0:T(8,128)}, f32[8,512]{1,0:T(8,128)}) custom-call(s32[2,2,256]{2,1,0:T(2,128)} %bitcast.19, s32[2,2,256]{2,1,0:T(2,128)} %bitcast.20, s32[2,256]{1,0:T(2,128)} %bitcast.21, s32[2,256]{1,0:T(2,128)} %bitcast.22, s32[2,256]{1,0:T(2,128)} %bitcast.23, ...), custom_call_target="tpu_custom_call" | custom-call | tf_op jit(solution)/shard_map/window/pallas_call | solution.py:638
  140.1 2.7 %hand_on.1 = (bf16[2048,512]{1,0:T(8,128)(2,1)}, bf16[2,256,512]{2,1,0:T(8,128)(2,1)}, f32[8,512]{1,0:T(8,128)}, f32[8,1024]{1,0:T(8,128)}, f32[8,512]{1,0:T(8,128)}) custom-call(bf16[2048,512]{1,0:T(8,128)(2,1)} %get-tuple-element.15.refs_0_, bf16[2,256,512]{2,1,0:T(8,128)(2,1)} %get-tuple-element.16.refs_1_, f32[8,512]{1,0:T(8,128)} %get-tuple-element.17.refs_2_, ...), custom_call_target="tpu_custom_call" | custom-call | tf_op jit(solution)/shard_map/hand_on/pallas_call | solution.py:719

commit v2 on v1

--- a/solution.py
+++ b/solution.py
@@ -112,6 +112,7 @@
     r3,
     h4,
     r4,
+    fin,
     send_sem,
     recv_sem,
 ):
@@ -125,10 +126,10 @@
     wide = width // 2
     me = lax.axis_index("mem")
     x = lax.axis_index("rep")
-    z = me // PLANE
-    yc = me % PLANE
-    y = yc // 2
-    c = yc % 2
+    z = lax.div(me, PLANE)
+    yc = lax.rem(me, PLANE)
+    y = lax.div(yc, 2)
+    c = lax.rem(yc, 2)
 
     loads = {}
     for at, (name, src, dst) in enumerate(
@@ -155,41 +156,35 @@
 
     @pl.loop(1, n)
     def _(k):
-        pl.semaphore_signal(barrier, inc=1, device_id={"mem": (me + k) % n}, device_id_type=MESH)
+        pl.semaphore_signal(barrier, inc=1, device_id={"mem": lax.rem(me + k, n)}, device_id_type=MESH)
 
     for k in range(1, nx):
         pl.semaphore_signal(barrier, inc=1, device_id={"rep": (x + k) % nx}, device_id_type=MESH)
 
-    @pl.loop(1, nz)
-    def _(k):
-        for j in range(1, nx):
-            pl.semaphore_signal(
-                barrier,
-                inc=1,
-                device_id={"mem": (z + k) % nz * PLANE + yc, "rep": (x + j) % nx},
-                device_id_type=MESH,
-            )
-
     def group_at(i):
-        h = (i + 1) // 2
-        return nz // 2 + h * (1 - 2 * (i % 2))
+        h = lax.div(i + 1, 2)
+        return nz // 2 + h * (1 - 2 * lax.rem(i, 2))
 
     def start_group(src, dst, g, sem):
-        @pl.loop(0, PLANE)
-        def _(j):
-            @pl.when(g * PLANE + j > 0)
-            def _():
-                q = g * PLANE + (j + yc) % PLANE
-                other = (q + z * PLANE) % n
-                mine = (me + n - (other // PLANE) * PLANE) % n
+        there = lax.rem(g + z, nz) * PLANE
+        mine = lax.rem(nz - g, nz) * PLANE + yc
+        for j in range(PLANE):
+            turned = lax.rem(yc + j, PLANE)
+
+            def send(turned=turned):
                 pltpu.make_async_remote_copy(
-                    src_ref=src(q),
+                    src_ref=src(g * PLANE + turned),
                     dst_ref=dst(mine),
                     send_sem=send_sem.at[sem],
                     recv_sem=recv_sem.at[sem],
-                    device_id={"mem": other},
+                    device_id={"mem": there + turned},
                     device_id_type=MESH,
                 ).start()
+
+            if j:
+                send()
+            else:
+                pl.when(g > 0)(send)
 
     def columns(t):
         return pl.ds(t * wide, wide)
@@ -225,7 +220,7 @@
         found = nt(marks_bf, high) * 64.0 + nt(marks_bf, low)
         ids_out[:, :, b * 128 : (b + 1) * 128] = (found.astype(I32) - 1).reshape(n, 1, 128)
 
-    pl.semaphore_wait(barrier, n - 1 + (nx - 1) * nz)
+    pl.semaphore_wait(barrier, n - 1 + nx - 1)
 
     @pl.loop(0, nz)
     def _(i):
@@ -233,9 +228,8 @@
 
     ids_in[pl.ds(yc, 1)] = ids_out[pl.ds(yc, 1)]
     wait_got(ids_in.at[pl.ds(0, n - 1)], 0)
-    wait_sent(ids_out.at[pl.ds(0, n - 1)], 0)
-
-    for b in range(2):
+
+    def spread(b):
         seen = ids_in[:, :, b * 128 : (b + 1) * 128].reshape(n, 128).astype(F32)
         mine = (iota((n, 128), 0) % PLANE) == (iota((n, 128), 1) // CAP)
         packed = jnp.sum(jnp.where(mine, seen, 0.0).reshape(nz, PLANE, 128), axis=1)
@@ -342,35 +336,33 @@
             rows_ref[b, 0, :, columns(t)] = got[:events]
             rows_ref[b, 1, :, columns(t)] = got[events:]
 
-    def update(b):
-        for t in range(2):
-
-            @pl.loop(0, 2)
-            def _(k):
-                state = rows_ref[b, k]
-                partner = rows_ref[b, 1 - k]
-                part = [slice(i * width + t * wide, i * width + (t + 1) * wide) for i in range(3)]
-                reset = sigmoid(nn(partner, gi_ref[:, part[0]]) + nn(state, gh_ref[:, part[0]]))
-                keep = sigmoid(nn(partner, gi_ref[:, part[1]]) + nn(state, gh_ref[:, part[1]]))
-                candidate = jnp.tanh(nn(partner, gi_ref[:, part[2]]) + reset * nn(state, gh_ref[:, part[2]]))
-                old = rows_ref[b, k, :, columns(t)].astype(F32)
-                upd_ref[pl.ds(pl.multiple_of(k * events, events), events), columns(t)] = (
-                    candidate + keep * (old - candidate)
-                ).astype(BF)
-
-            @pl.loop(0, nz // per)
-            def _(i):
-                groups, where = places(i)
-                pick = jnp.concatenate([pickt_ref[at, :] for at in where], axis=0)
-                got = nn(pick, upd_ref[:, columns(t)]).astype(BF)
-                for k in range(per):
-                    outgoing[b, where[k], columns(t)] = got[k * GROUP : (k + 1) * GROUP]
-                for k in range(per):
-                    start_group(block(outgoing, b, t), block(arrived, b, t), groups[k], 5 + 2 * b + t)
-
-            own_block(outgoing, arrived, b, t)
-
-    def apply(b, t, source, target):
+    def update(b, t):
+        @pl.loop(0, 2)
+        def _(k):
+            state = rows_ref[b, k]
+            partner = rows_ref[b, 1 - k]
+            gate = [slice(i * width + t * wide, i * width + (t + 1) * wide) for i in range(3)]
+            reset = sigmoid(nn(partner, gi_ref[:, gate[0]]) + nn(state, gh_ref[:, gate[0]]))
+            keep = sigmoid(nn(partner, gi_ref[:, gate[1]]) + nn(state, gh_ref[:, gate[1]]))
+            candidate = jnp.tanh(nn(partner, gi_ref[:, gate[2]]) + reset * nn(state, gh_ref[:, gate[2]]))
+            old = rows_ref[b, k, :, columns(t)].astype(F32)
+            upd_ref[pl.ds(pl.multiple_of(k * events, events), events), columns(t)] = (
+                candidate + keep * (old - candidate)
+            ).astype(BF)
+
+        @pl.loop(0, nz // per)
+        def _(i):
+            groups, where = places(i)
+            pick = jnp.concatenate([pickt_ref[at, :] for at in where], axis=0)
+            got = nn(pick, upd_ref[:, columns(t)]).astype(BF)
+            for k in range(per):
+                outgoing[b, where[k], columns(t)] = got[k * GROUP : (k + 1) * GROUP]
+            for k in range(per):
+                start_group(block(outgoing, b, t), block(arrived, b, t), groups[k], 5 + 2 * b + t)
+
+        own_block(outgoing, arrived, b, t)
+
+    def apply(b, t, source, target, store=None):
         wait_got(others(arrived, b, t), 5 + 2 * b + t)
 
         @pl.loop(0, nodes // step)
@@ -380,57 +372,88 @@
             inverse = inverse_ref[at, 0:1]
             old = source[at, columns(t)].astype(F32)
             target[at, columns(t)] = jnp.where(inverse > 0, sums * inverse, old).astype(BF)
+            if store:
+                store(k).start()
 
     def store_memory(k):
-        at = pl.ds(k * step, step)
+        at = pl.ds(pl.multiple_of(k * step, step), step)
         return pltpu.make_async_copy(newmem_ref.at[at], newmem_hbm.at[at], out_sem.at[2 + k])
 
     def store_embeddings(b):
         return pltpu.make_async_copy(emb_ref.at[b], emb_hbm.at[b], out_sem.at[b])
 
+    scale = 1.0 / math.sqrt(half_width)
+
+    def head_query(head):
+        return q_ref[:, pair_columns(head // 2)] * half_lanes(head % 2, scale)
+
+    def head_rows(head, base=0):
+        return pl.ds(base + head * half_width, half_width)
+
+    def add_grad(b, ref, cols, grad):
+        ref[:, cols] = grad if b == 0 else ref[:, cols] + grad
+
     def attend(b):
-        source = rows_ref[b, 0]
-        cot = cot_ref[b]
-        q_ref[...] = nn(source, wq_ref[...]).astype(BF)
-        scale = 1.0 / math.sqrt(half_width)
-
-        for pair in range(HEADS // 2):
-            cols = pair_columns(pair)
-            vcols = pair_columns(pair, width)
-            dk = jnp.zeros((nbrs, 2 * half_width), F32)
-            dv = jnp.zeros((nbrs, 2 * half_width), F32)
-            for half in range(2):
-                head = 2 * pair + half
-                q = q_ref[:, cols] * half_lanes(half, scale)
-                d = datt_ref[:, cols] * half_lanes(half, 1.0)
-                logits = nt(kv_ref[:, cols], q) + bias_ref[head]
-                weighted = jnp.exp(logits - jnp.max(logits, axis=0, keepdims=True))
-                weights = weighted * (1.0 / jnp.sum(weighted, axis=0, keepdims=True))
-                w = weights.astype(BF)
-                at = pl.ds(head * half_width, half_width)
-                vat = pl.ds(width + head * half_width, half_width)
-                att_ref[at, :] = nn(kvt_ref[vat, :], w).astype(BF)
-                dw = dw_ref[head]
-                inner = jnp.sum(dw * weights, axis=0, keepdims=True)
-                dl = (weights * (dw - inner)).astype(BF)
-                dq_ref[at, :] = (nn(kvt_ref[at, :], dl) * scale).astype(BF)
-                dv = dv + nn(w, d)
-                dk = dk + nn(dl, q)
-            dkv_ref[:, cols] = dk.astype(BF)
-            dkv_ref[:, vcols] = dv.astype(BF)
-
-        emb_ref[b] = (source.astype(F32) + nn(att_ref[...].T, wo_ref[...])).astype(BF)
-        go = nn(att_ref[...], cot)
-        gq = nn(source.T, dq_ref[...].T)
-        gkv = nn(feat_ref[b].T, dkv_ref[...])
-        if b == 0:
-            ga_ref[:, :width] = gq
-            ga_ref[:, width:] = go
-            gb_ref[...] = gkv
-        else:
-            ga_ref[:, :width] += gq
-            ga_ref[:, width:] += go
-            gb_ref[...] += gkv
+        q_ref[...] = nn(rows_ref[b, 0], wq_ref[...]).astype(BF)
+
+        def score(head):
+            return nt(kv_ref[:, pair_columns(head // 2)], head_query(head)) + bias_ref[head]
+
+        def weigh(head, logits):
+            weighted = jnp.exp(logits - jnp.max(logits, axis=0, keepdims=True))
+            weights = weighted * (1.0 / jnp.sum(weighted, axis=0, keepdims=True))
+            bias_ref[head] = weights
+            return weights.astype(BF)
+
+        def combine(head, w, held):
+            att_ref[head_rows(head), :] = nn(kvt_ref[head_rows(head, width), :], w).astype(BF)
+            d = datt_ref[:, pair_columns(head // 2)] * half_lanes(head % 2, 1.0)
+            dv = nn(w, d)
+            if head % 2 == 0:
+                return dv
+            dkv_ref[:, pair_columns(head // 2, width)] = (held + dv).astype(BF)
+
+        logits = score(0)
+        ready = held = None
+        for head in range(HEADS):
+            ahead = score(head + 1) if head + 1 < HEADS else None
+            if head:
+                held = combine(head - 1, ready, held)
+            ready = weigh(head, logits)
+            logits = ahead
+        combine(HEADS - 1, ready, held)
+        values = pl.ds(width, width)
+        add_grad(b, ga_ref, values, nn(att_ref[...], cot_ref[b]))
+        add_grad(b, gb_ref, values, nn(feat_ref[b].T, dkv_ref[:, values]))
+
+    def attend_back(b):
+        def weigh(head):
+            weights = bias_ref[head]
+            dw = dw_ref[head]
+            inner = jnp.sum(dw * weights, axis=0, keepdims=True)
+            return (weights * (dw - inner)).astype(BF)
+
+        def combine(head, dl, held):
+            dq_ref[head_rows(head), :] = (nn(kvt_ref[head_rows(head), :], dl) * scale).astype(BF)
+            dk = nn(dl, head_query(head))
+            if head % 2 == 0:
+                return dk
+            dkv_ref[:, pair_columns(head // 2)] = (held + dk).astype(BF)
+
+        ready = held = None
+        for head in range(HEADS):
+            if head:
+                held = combine(head - 1, ready, held)
+            ready = weigh(head)
+        combine(HEADS - 1, ready, held)
+        keys = pl.ds(0, width)
+        add_grad(b, ga_ref, keys, nn(rows_ref[b, 0].T, dq_ref[...].T))
+        add_grad(b, gb_ref, keys, nn(feat_ref[b].T, dkv_ref[:, keys]))
+
+    def embed(b):
+        source = rows_ref[b, 0].astype(F32)
+        emb_ref[b] = (source + nn(att_ref[...].T, wo_ref[...])).astype(BF)
+        store_embeddings(b).start()
 
     part = 2 * width // n
     plane = nz * part
@@ -455,17 +478,15 @@
     def reduce_core(t):
         share = part // 2
 
-        @pl.loop(0, n)
-        def _(d):
-            zz = d // PLANE
-            yy = (d % PLANE) // 2
-            cc = d % 2
-            rows = pl.ds(pl.multiple_of(d * share, share), share)
+        @pl.loop(0, nz)
+        def _(zz):
             cols = pl.ds(t * width, width)
-            both = jnp.concatenate([ga_ref[rows, cols], gb_ref[rows, cols]], axis=0).astype(BF)
-            at = pl.ds(pl.multiple_of((yy * nz + zz) * part, part), part)
-            for k in range(nx):
-                h1[t, cc, k, at, :] = both[:, k * cut : (k + 1) * cut]
+            for j in range(PLANE):
+                rows = pl.ds(pl.multiple_of((zz * PLANE + j) * share, share), share)
+                both = jnp.concatenate([ga_ref[rows, cols], gb_ref[rows, cols]], axis=0).astype(BF)
+                at = pl.ds(pl.multiple_of((j // 2 * nz + zz) * part, part), part)
+                for k in range(nx):
+                    h1[t, j % 2, k, at, :] = both[:, k * cut : (k + 1) * cut]
 
         copy_to(h1.at[t, 1 - c], r1.at[t], {"mem": me + 1 - 2 * c}, 9 + t)
 
@@ -495,66 +516,69 @@
             for k in range(NY - 1):
                 total = total + r3[t, k].astype(F32)
             h4[:, t * cut : (t + 1) * cut] = total.astype(BF)
-        here = r4.at[z * nx + x]
-        here[...] = h4[rows_of_z(z), :]
+        for k in range(1, nz):
+            zz = lax.rem(z + k, nz)
+            copy_to(h4.at[rows_of_z(zz)], r4.at[k - 1], {"mem": zz * PLANE + yc}, 15)
+
+    def share_x():
+        total = h4[rows_of_z(z), :].astype(F32)
+        if nz > 1:
+            wait_got(r4, 15)
+            for k in range(nz - 1):
+                total = total + r4[k].astype(F32)
+        fin[x] = total
         for k in range(1, nx):
-            copy_to(h4.at[rows_of_z(z)], here, {"rep": (x + k) % nx}, 15)
-
-        @pl.loop(1, nz)
-        def _(k):
-            zz = (z + k) % nz
-            for j in range(nx):
-                there = {"mem": zz * PLANE + yc, "rep": (x + j) % nx} if j else {"mem": zz * PLANE + yc}
-                copy_to(h4.at[rows_of_z(zz)], here, there, 15)
-
-    def all_but_one():
-        return r4.at[pl.ds(0, nz * nx - 1)]
+            copy_to(fin.at[x], fin.at[x], {"rep": lax.rem(x + k, nx)}, 16)
 
     def finish():
-        wait_got(all_but_one(), 15)
+        if nx > 1:
+            wait_got(fin.at[pl.ds(0, nx - 1)], 16)
         share = part // 2
         for k in range(nx):
-            total = r4[k].astype(F32)
-            for j in range(1, nz):
-                total = total + r4[j * nx + k].astype(F32)
+            total = fin[k]
             at = slice(k * cut, (k + 1) * cut)
             gq_ref[:, at] = total[:share, :cut]
             go_ref[:, at] = total[:share, cut:]
             gkv_ref[:, at] = total[share:, :cut]
             gkv_ref[:, width + k * cut : width + (k + 1) * cut] = total[share:, cut:]
 
+    spread(0)
     loaded("mem")
     serve(0, 0, mem_ref)
     serve(0, 1, mem_ref)
+    spread(1)
     loaded("nidx", "feat", "wkv", "wo", "cot")
     prepare(0)
     name_rows(0)
     ask_all(1)
     loaded("gi", "gh", "wq")
     fetch(0)
-    update(0)
+    update(0, 0)
+    update(0, 1)
     attend(0)
-    store_embeddings(0).start()
+    attend_back(0)
+    embed(0)
     for t in range(2):
         apply(0, t, mem_ref, mem1)
         serve(1, t, mem1)
     prepare(1)
     name_rows(1)
     fetch(1)
-    update(1)
+    update(1, 0)
     attend(1)
-    store_embeddings(1).start()
+    reduce_core(1)
+    attend_back(1)
+    reduce_x(1)
     reduce_core(0)
-    reduce_core(1)
+    update(1, 1)
     reduce_x(0)
-    reduce_x(1)
+    embed(1)
     apply(1, 0, mem1, newmem_ref)
+    reduce_y(1)
     reduce_y(0)
-    reduce_y(1)
     reduce_z()
-    apply(1, 1, mem1, newmem_ref)
-    for k in range(nodes // step):
-        store_memory(k).start()
+    apply(1, 1, mem1, newmem_ref, store_memory)
+    share_x()
     finish()
 
     for b in range(2):
@@ -562,12 +586,16 @@
             wait_sent(others(served, b, t), 1 + 2 * b + t)
             wait_sent(others(outgoing, b, t), 5 + 2 * b + t)
         store_embeddings(b).wait()
+    wait_sent(ids_out.at[pl.ds(0, n - 1)], 0)
     for t in range(2):
         wait_sent(r1.at[t], 9 + t)
         if nx > 1:
             wait_sent(r2.at[t], 11 + t)
         wait_sent(r3.at[t], 13 + t)
-    wait_sent(all_but_one(), 15)
+    if nz > 1:
+        wait_sent(r4, 15)
+    if nx > 1:
+        wait_sent(fin.at[pl.ds(0, nx - 1)], 16)
     for k in range(nodes // step):
         store_memory(k).wait()
 
@@ -578,7 +606,7 @@
     steps = []
     for src, dst, held in zip(refs[:count], refs[count : 2 * count], refs[2 * count : 3 * count]):
         rows = src.shape[0]
-        pieces = 4 if rows % 128 == 0 else 1
+        pieces = 8 if rows % 128 == 0 else 1
         for k in range(pieces):
             at = pl.ds(k * (rows // pieces), rows // pieces)
             get = pltpu.make_async_copy(src.at[at], held.at[at], sem.at[0, len(steps)])
@@ -691,9 +719,10 @@
             pltpu.VMEM((2, half, cut), BF),
             pltpu.VMEM((2, NY - 1, plane, cut), BF),
             pltpu.VMEM((plane, 2 * cut), BF),
-            pltpu.VMEM((nz * nx, part, 2 * cut), BF),
-            pltpu.SemaphoreType.DMA((16,)),
-            pltpu.SemaphoreType.DMA((16,)),
+            pltpu.VMEM((max(nz - 1, 1), part, 2 * cut), BF),
+            pltpu.VMEM((nx, part, 2 * cut), F32),
+            pltpu.SemaphoreType.DMA((17,)),
+            pltpu.SemaphoreType.DMA((17,)),
         ],
         compiler_params=pltpu.CompilerParams(
             collective_id=0, has_side_effects=True, vmem_limit_bytes=60 * 1024 * 1024
@@ -721,7 +750,7 @@
         out_shape=outputs,
         in_specs=[hbm] * 5,
         out_specs=(hbm,) * 5,
-        scratch_shapes=[pltpu.VMEM(out.shape, out.dtype) for out in outputs] + [pltpu.SemaphoreType.DMA((2, 8))],
+        scratch_shapes=[pltpu.VMEM(out.shape, out.dtype) for out in outputs] + [pltpu.SemaphoreType.DMA((2, 16))],
         compiler_params=pltpu.CompilerParams(vmem_limit_bytes=60 * 1024 * 1024),
         name="hand_on",
     )(*results)

time: 143 us -> 137 us (0.958)
  Pallas kernels: 142 us -> 136 us
    pallas_call x1, Pallas kernels: 139 us -> 134 us  [on_device(): pl.pallas_call(functools.partial(window, nx), out_shape=outputs, in_specs...]
where the time goes in v2:
time: 137 us
  Pallas kernels  136 us (99%)
    pallas_call x1, Pallas kernels, on_device(): pl.pallas_call(functools.partial(window, nx), out_shape=outputs, in_specs...  134 us
    pallas_call x1, Pallas kernels, on_device(): pl.pallas_call(hand_on, out_shape=outputs, in_specs=[hbm] * 5, out_specs=...  2.76 us

profile of v2, /device:TPU:1, one launch (start us, length us, event | category | flops | bytes accessed | tf_op | source)
XLA Modules:
  0.0 137.1 jit_solution(7175289283550064693)
XLA Ops:
  0.6 133.5 %window.1 = (bf16[2048,512]{1,0:T(8,128)(2,1)}, bf16[2,256,512]{2,1,0:T(8,128)(2,1)}, f32[8,512]{1,0:T(8,128)}, f32[8,1024]{1,0:T(8,128)}, f32[8,512]{1,0:T(8,128)}) custom-call(s32[2,2,256]{2,1,0:T(2,128)} %bitcast.19, s32[2,2,256]{2,1,0:T(2,128)} %bitcast.20, s32[2,256]{1,0:T(2,128)} %bitcast.21, s32[2,256]{1,0:T(2,128)} %bitcast.22, s32[2,256]{1,0:T(2,128)} %bitcast.23, ...), custom_call_target="tpu_custom_call" | custom-call | tf_op jit(solution)/shard_map/window/pallas_call | solution.py:666
  134.2 2.8 %hand_on.1 = (bf16[2048,512]{1,0:T(8,128)(2,1)}, bf16[2,256,512]{2,1,0:T(8,128)(2,1)}, f32[8,512]{1,0:T(8,128)}, f32[8,1024]{1,0:T(8,128)}, f32[8,512]{1,0:T(8,128)}) custom-call(bf16[2048,512]{1,0:T(8,128)(2,1)} %get-tuple-element.15.refs_0_, bf16[2,256,512]{2,1,0:T(8,128)(2,1)} %get-tuple-element.16.refs_1_, f32[8,512]{1,0:T(8,128)} %get-tuple-element.17.refs_2_, ...), custom_call_target="tpu_custom_call" | custom-call | tf_op jit(solution)/shard_map/hand_on/pallas_call | solution.py:748

commit v3 on v2

--- a/solution.py
+++ b/solution.py
@@ -568,17 +568,17 @@
     attend(1)
     reduce_core(1)
     attend_back(1)
+    reduce_core(0)
     reduce_x(1)
-    reduce_core(0)
     update(1, 1)
     reduce_x(0)
     embed(1)
-    apply(1, 0, mem1, newmem_ref)
     reduce_y(1)
     reduce_y(0)
+    apply(1, 0, mem1, newmem_ref)
     reduce_z()
+    share_x()
     apply(1, 1, mem1, newmem_ref, store_memory)
-    share_x()
     finish()
 
     for b in range(2):

time: 137 us -> 136 us (level)
    pallas_call x1, Pallas kernels: 134 us -> 132 us  [on_device(): pl.pallas_call(functools.partial(window, nx), out_shape=outputs, in_specs...]
where the time goes in v3:
time: 136 us
  Pallas kernels  135 us (99%)
    pallas_call x1, Pallas kernels, on_device(): pl.pallas_call(functools.partial(window, nx), out_shape=outputs, in_specs...  132 us
    pallas_call x1, Pallas kernels, on_device(): pl.pallas_call(hand_on, out_shape=outputs, in_specs=[hbm] * 5, out_specs=...  2.76 us

profile of v3, /device:TPU:1, one launch (start us, length us, event | category | flops | bytes accessed | tf_op | source)
XLA Modules:
  0.0 135.5 jit_solution(4922606000210499829)
XLA Ops:
  0.6 132.0 %window.1 = (bf16[2048,512]{1,0:T(8,128)(2,1)}, bf16[2,256,512]{2,1,0:T(8,128)(2,1)}, f32[8,512]{1,0:T(8,128)}, f32[8,1024]{1,0:T(8,128)}, f32[8,512]{1,0:T(8,128)}) custom-call(s32[2,2,256]{2,1,0:T(2,128)} %bitcast.19, s32[2,2,256]{2,1,0:T(2,128)} %bitcast.20, s32[2,256]{1,0:T(2,128)} %bitcast.21, s32[2,256]{1,0:T(2,128)} %bitcast.22, s32[2,256]{1,0:T(2,128)} %bitcast.23, ...), custom_call_target="tpu_custom_call" | custom-call | tf_op jit(solution)/shard_map/window/pallas_call | solution.py:666
  132.6 2.8 %hand_on.1 = (bf16[2048,512]{1,0:T(8,128)(2,1)}, bf16[2,256,512]{2,1,0:T(8,128)(2,1)}, f32[8,512]{1,0:T(8,128)}, f32[8,1024]{1,0:T(8,128)}, f32[8,512]{1,0:T(8,128)}) custom-call(bf16[2048,512]{1,0:T(8,128)(2,1)} %get-tuple-element.15.refs_0_, bf16[2,256,512]{2,1,0:T(8,128)(2,1)} %get-tuple-element.16.refs_1_, f32[8,512]{1,0:T(8,128)} %get-tuple-element.17.refs_2_, ...), custom_call_target="tpu_custom_call" | custom-call | tf_op jit(solution)/shard_map/hand_on/pallas_call | solution.py:748
